TPU v7x, 256 devices: a whole 4x4x8 slice. The times are simulated.
256 devices in a mesh: tm: 64 (over z, x, core), tensor: 4 (over y).
Axes of the slice: x: 4, y: 4, z: 8, core: 2. Of those that a mesh axis runs over, the one named last changes fastest.
Arguments:
- enc_frames: bfloat16 [96000, 1280], P('tm'), may hold values from -1.5 to 1.5
- span_counts: int32 [8], replicated, may hold values from 1 to 16, 64 in all
- enc_gain: float32 [1280], replicated, may hold values from 0.1 to 1.9
- enc_wq: bfloat16 [1280, 1024], P(None, 'tensor'), as said below
- enc_wk: bfloat16 [1280, 1024], P(None, 'tensor'), as said below
- enc_wv: bfloat16 [1280, 1024], P(None, 'tensor'), may hold values from -0.15625 to 0.15625
- enc_wo: bfloat16 [1024, 1280], P('tensor'), may hold values from -0.1875 to 0.1875
- adapter: bfloat16 [1280, 3584], P(None, 'tensor'), may hold values from -0.15625 to 0.15625
- owner_map: int32 [24000, 1], replicated, may hold values from 0 to 63; in each aligned block of 375 rows (0 to 374, 375 to 749, ...) at most 7 rows name the same one
- text_embeds: bfloat16 [4096, 3584], P('tm'), may hold values from -6 to 6
- llm_gain: float32 [3584], replicated, may hold values from 0.1 to 1.9
- llm_wq: bfloat16 [3584, 3584], P('tm', 'tensor'), as said below
- llm_wk: bfloat16 [3584, 512], P('tm', 'tensor'), as said below
- llm_wv: bfloat16 [3584, 512], P('tm', 'tensor'), may hold values from -0.09375 to 0.09375
- llm_bq: float32 [3584], P('tensor'), may hold values from -3 to 3
- llm_bk: float32 [512], P('tensor'), may hold values from -3 to 3
- llm_bv: float32 [512], P('tensor'), may hold values from -3 to 3
Outputs:
- context: bfloat16 [32768, 3584], P('tm', 'tensor')
Inputs may be any that keep to these rules, and one draw needn't show every extreme that they name: `owner_map`: in each aligned block of 375 rows (the pooled frames of one device along tm), no owner is named by more than 7 rows. `span_counts`: the counts sum to 64. `enc_wq`: A projection matrix scaled by the inverse square root of its fan-in. `enc_wk`: A projection matrix scaled by the inverse square root of its fan-in. `llm_wq`: A projection matrix scaled by the inverse square root of its fan-in. `llm_wk`: A projection matrix scaled by the inverse square root of its fan-in.
All inputs are finite; a program needn't handle non-finite values.
Results may differ from a plain program's by a relative error of at most 0.03.
Values may be sent and summed in bfloat16 or wider, within the bound.
A program may use at most 128 MiB of HBM per device.

v0:
```python
import functools
import math

import jax
import jax.numpy as jnp
from jax import lax
from jax.experimental import pallas as pl
from jax.experimental.pallas import tpu as pltpu
from jax.sharding import PartitionSpec as P

B16 = jnp.bfloat16
F32 = jnp.float32
MESH = pl.DeviceIdType.MESH

ENC_HD = 64
FRAMES = 1500
POOL = 4
LLM_HD = 128
PAD = 1536
ROWS = 384
TILES = PAD // ROWS
PROWS = ROWS // POOL
POOLED = PAD // POOL
SLOT = 8
FEAT = 320
WIDE = 384
LOG2E = math.log2(math.e)


def dot(a, b):
    return jnp.dot(a, b, preferred_element_type=F32)


def encoder_kernel(
    n_tm,
    n_t,
    frames_ref,
    gain_ref,
    wq_ref,
    wk_ref,
    wv_ref,
    wo_ref,
    target_ref,
    open_ref,
    x_ref,
    tail_ref,
    q_ref,
    kt_ref,
    v_ref,
    ktp_ref,
    vp_ref,
    vm_ref,
    o1_ref,
    m1_ref,
    l1_ref,
    res_ref,
    part_ref,
    rs_ref,
    slots_ref,
    got_ref,
    kv_send,
    kv_recv,
    rs_send,
    rs_recv,
    a2a_send,
    a2a_recv,
    ag_send,
    ag_recv,
):
    me = lax.axis_index("tm")
    t = lax.axis_index("tensor")
    lane = lax.broadcasted_iota(jnp.int32, (1, 256), 1) // ENC_HD
    heads = 256 // ENC_HD

    barrier = pltpu.get_barrier_semaphore()

    def greet(k, _):
        pl.semaphore_signal(
            barrier, inc=1, device_id=(lax.rem(me + k, n_tm), t), device_id_type=MESH
        )
        return 0

    lax.fori_loop(1, n_tm, greet, 0)
    for k in range(1, n_t):
        pl.semaphore_signal(
            barrier, inc=1, device_id=(me, lax.rem(t + k, n_t)), device_id_type=MESH
        )

    tail_ref[...] = jnp.zeros_like(tail_ref)
    tail_ref[0 : FRAMES - 1280, :] = frames_ref[1280:FRAMES, :]
    prow = lax.broadcasted_iota(jnp.int32, (64, 256), 0)
    pcol = lax.broadcasted_iota(jnp.int32, (64, 256), 1)
    pool = jnp.where(pcol // POOL == prow, 0.25, 0.0).astype(B16)

    def project(raw, i):
        rows = pl.ds(pl.multiple_of(i * 256, 256), 256)
        x = raw.astype(F32)
        mean = jnp.mean(x, axis=-1, keepdims=True)
        cent = x - mean
        var = jnp.mean(cent * cent, axis=-1, keepdims=True)
        normed = (cent * lax.rsqrt(var + 1e-05) * gain_ref[...]).astype(B16)
        q_ref[rows, :] = (dot(normed, wq_ref[...]) * (ENC_HD**-0.5 * LOG2E)).astype(B16)
        kt_ref[:, rows] = jnp.transpose(dot(normed, wk_ref[...])).astype(B16)
        v_ref[rows, :] = dot(normed, wv_ref[...]).astype(B16)
        res = dot(pool, raw)
        prows = pl.ds(pl.multiple_of(i * 64, 64), 64)
        for tt in range(n_t):

            @pl.when(t == tt)
            def _():
                res_ref[prows, :] = res[:, tt * FEAT : (tt + 1) * FEAT]

    def project_block(i, _):
        project(frames_ref[pl.ds(pl.multiple_of(i * 256, 256), 256), :], i)
        return 0

    lax.fori_loop(0, 5, project_block, 0)
    project(tail_ref[...], 5)

    pl.semaphore_wait(barrier, n_tm - 1 + n_t - 1)

    def passed(src, dst, k):
        return pltpu.make_async_remote_copy(
            src_ref=src,
            dst_ref=dst,
            send_sem=kv_send.at[k],
            recv_sem=kv_recv.at[k],
            device_id=(lax.rem(me + 1, n_tm), t),
            device_id_type=MESH,
        )

    keys_on = passed(kt_ref, ktp_ref, 0)
    values_on = passed(v_ref, vp_ref, 1)
    keys_on.start()
    values_on.start()

    tail_lane = lax.broadcasted_iota(jnp.int32, (1, 128), 1) < FRAMES - (PAD - 128)

    def head_masks(values):
        for h in range(heads):
            vm_ref[h] = jnp.where(lane == h, values, jnp.ones((), B16))

    def half(rows, keys_ref):
        q = q_ref[rows, :]
        out = jnp.zeros((ROWS, 256), F32)
        top = jnp.zeros((ROWS, 256), F32)
        den = jnp.zeros((ROWS, 256), F32)
        for h in range(heads):
            s = dot(jnp.where(lane == h, q, jnp.zeros_like(q)), keys_ref[...])
            s = jnp.concatenate(
                [s[:, : PAD - 128], jnp.where(tail_lane, s[:, PAD - 128 :], -1e30)], axis=1
            )
            m = jnp.max(s, axis=1, keepdims=True)
            p = jnp.exp2(s - m).astype(B16)
            o = dot(p, vm_ref[h])
            col = 255 if h < heads - 1 else 0
            out = jnp.where(lane == h, o, out)
            top = jnp.where(lane == h, m, top)
            den = jnp.where(lane == h, o[:, col : col + 1], den)
        return out, top, den

    head_masks(v_ref[...])

    def own_half(i, _):
        rows = pl.ds(pl.multiple_of(i * ROWS, ROWS), ROWS)
        out, top, den = half(rows, kt_ref)
        o1_ref[rows, :] = out
        m1_ref[rows, :] = top
        l1_ref[rows, :] = den
        return 0

    lax.fori_loop(0, TILES, own_half, 0)

    keys_on.wait()
    values_on.wait()
    head_masks(vp_ref[...])
    is_open = open_ref[0, 0] > 0
    trow = lax.broadcasted_iota(jnp.int32, (PROWS, ROWS), 0)
    tcol = lax.broadcasted_iota(jnp.int32, (PROWS, ROWS), 1)
    tile_pool = jnp.where(tcol // POOL == trow, 0.25, 0.0).astype(B16)

    def summed(i, k):
        rows = pl.ds(pl.multiple_of(i * PROWS, PROWS), PROWS)
        to = lax.rem(t + k, n_t)
        return pltpu.make_async_remote_copy(
            src_ref=part_ref.at[to, rows],
            dst_ref=rs_ref.at[t, rows],
            send_sem=rs_send.at[i, k - 1],
            recv_sem=rs_recv.at[i, k - 1],
            device_id=(me, to),
            device_id_type=MESH,
        )

    def prior_half(i, _):
        rows = pl.ds(pl.multiple_of(i * ROWS, ROWS), ROWS)
        out, top, den = half(rows, ktp_ref)
        m1 = m1_ref[rows, :]
        both = jnp.where(is_open, m1, jnp.maximum(m1, top))
        w1 = jnp.exp2(m1 - both)
        w2 = jnp.where(is_open, 0.0, jnp.exp2(jnp.minimum(top - both, 0.0)))
        total = w1 * l1_ref[rows, :] + w2 * den
        ctx = ((w1 * o1_ref[rows, :] + w2 * out) / total).astype(B16)
        pooled = dot(tile_pool, ctx).astype(B16)
        partial = dot(pooled, wo_ref[...]).astype(B16)
        prows = pl.ds(pl.multiple_of(i * PROWS, PROWS), PROWS)
        for tt in range(n_t):
            part_ref[tt, prows, :] = partial[:, tt * FEAT : (tt + 1) * FEAT]
        for k in range(1, n_t):
            summed(i, k).start()
        return 0

    lax.fori_loop(0, TILES, prior_half, 0)

    def summed_wait(i, _):
        for k in range(1, n_t):
            summed(i, k).wait()
        return 0

    lax.fori_loop(0, TILES, summed_wait, 0)

    total = part_ref[t].astype(F32)
    for k in range(1, n_t):
        total = total + rs_ref[lax.rem(t + k, n_t)].astype(F32)
    pooled = (res_ref[...] + total).astype(B16)
    wide = jnp.concatenate([pooled, jnp.ones((POOLED, WIDE - FEAT), B16)], axis=1)
    slot_row = lax.broadcasted_iota(jnp.int32, (n_tm * SLOT, POOLED), 0)
    place = jnp.where(slot_row == target_ref[...], 1.0, 0.0).astype(B16)
    slots_ref[...] = dot(place, wide).reshape(n_tm, SLOT, WIDE).astype(B16)
    got_ref[me] = slots_ref[me]

    def routed(k):
        to = lax.rem(me + k, n_tm)
        return pltpu.make_async_remote_copy(
            src_ref=slots_ref.at[to],
            dst_ref=got_ref.at[me],
            send_sem=a2a_send,
            recv_sem=a2a_recv,
            device_id=(to, t),
            device_id_type=MESH,
        )

    def routed_start(k, _):
        routed(k).start()
        return 0

    lax.fori_loop(1, n_tm, routed_start, 0)
    many = slots_ref.at[pl.ds(0, n_tm - 1)]
    pltpu.make_async_copy(many, many, a2a_send).wait()
    many = got_ref.at[pl.ds(0, n_tm - 1)]
    pltpu.make_async_copy(many, many, a2a_recv).wait()

    def spread(k):
        return pltpu.make_async_remote_copy(
            src_ref=got_ref,
            dst_ref=x_ref.at[t],
            send_sem=ag_send.at[k - 1],
            recv_sem=ag_recv.at[k - 1],
            device_id=(me, lax.rem(t + k, n_t)),
            device_id_type=MESH,
        )

    for k in range(1, n_t):
        spread(k).start()
    x_ref[t] = got_ref[...]
    for k in range(1, n_t):
        spread(k).wait()


def run_encoder(n_tm, n_t, frames, gain, wq, wk, wv, wo, target, is_open):
    vmem = pl.BlockSpec(memory_space=pltpu.VMEM)
    smem = pl.BlockSpec(memory_space=pltpu.SMEM)
    return pl.pallas_call(
        functools.partial(encoder_kernel, n_tm, n_t),
        out_shape=jax.ShapeDtypeStruct((n_t, n_tm, SLOT, WIDE), B16),
        in_specs=[vmem] * 7 + [smem],
        out_specs=vmem,
        scratch_shapes=[
            pltpu.VMEM((256, frames.shape[1]), B16),
            pltpu.VMEM((PAD, 256), B16),
            pltpu.VMEM((256, PAD), B16),
            pltpu.VMEM((PAD, 256), B16),
            pltpu.VMEM((256, PAD), B16),
            pltpu.VMEM((PAD, 256), B16),
            pltpu.VMEM((256 // ENC_HD, PAD, 256), B16),
            pltpu.VMEM((PAD, 256), F32),
            pltpu.VMEM((PAD, 256), F32),
            pltpu.VMEM((PAD, 256), F32),
            pltpu.VMEM((POOLED, FEAT), F32),
            pltpu.VMEM((n_t, POOLED, FEAT), B16),
            pltpu.VMEM((n_t, POOLED, FEAT), B16),
            pltpu.VMEM((n_tm, SLOT, WIDE), B16),
            pltpu.VMEM((n_tm, SLOT, WIDE), B16),
            pltpu.SemaphoreType.DMA((2,)),
            pltpu.SemaphoreType.DMA((2,)),
            pltpu.SemaphoreType.DMA((TILES, n_t - 1)),
            pltpu.SemaphoreType.DMA((TILES, n_t - 1)),
            pltpu.SemaphoreType.DMA,
            pltpu.SemaphoreType.DMA,
            pltpu.SemaphoreType.DMA((n_t - 1,)),
            pltpu.SemaphoreType.DMA((n_t - 1,)),
        ],
        compiler_params=pltpu.CompilerParams(
            collective_id=0, has_side_effects=True, vmem_limit_bytes=56 << 20
        ),
        cost_estimate=pl.CostEstimate(
            flops=20_000_000_000, bytes_accessed=20_000_000, transcendentals=20_000_000
        ),
    )(frames, gain, wq, wk, wv, wo, target, is_open)


def root_norm(samples, norm_gain):
    power = jnp.mean(samples * samples, axis=-1, keepdims=True)
    return samples * lax.rsqrt(power + 1e-06) * norm_gain


def rotate(vectors, positions):
    half_width = vectors.shape[-1] // 2
    inv_freq = jnp.exp(
        jnp.arange(half_width, dtype=jnp.float32) * (-2.0 * math.log(1000000.0) / vectors.shape[-1])
    )
    angles = positions.astype(jnp.float32)[:, None] * inv_freq[None, :]
    cosine = jnp.cos(angles)
    sine_table = jnp.sin(angles)
    lower_half = vectors[..., :half_width]
    upper_half = vectors[..., half_width:]
    return jnp.concatenate(
        [
            lower_half * cosine - upper_half * sine_table,
            upper_half * cosine + lower_half * sine_table,
        ],
        axis=-1,
    )


def grouped_attention(query_heads, key_heads, value_heads, row_present, positions):
    head_width = query_heads.shape[-1]
    row_count = query_heads.shape[1]
    kv_count = key_heads.shape[0]
    grouped = query_heads.reshape(kv_count, -1, row_count, head_width)
    scores = jnp.einsum(
        "kgqd,ksd->kgqs", grouped, key_heads, preferred_element_type=jnp.float32
    ) * head_width ** (-0.5)
    allowed = (row_present[None, :] > 0) & (positions[None, :] <= positions[:, None]) | jnp.eye(
        row_count, dtype=bool
    )
    scores = jnp.where(allowed[None, None], scores, -1e30)
    peak = jnp.max(scores, axis=-1, keepdims=True)
    weights = jnp.exp(scores - peak)
    probabilities = (weights / jnp.sum(weights, axis=-1, keepdims=True)).astype(jnp.bfloat16)
    context = jnp.einsum(
        "kgqs,ksd->kgqd", probabilities, value_heads, preferred_element_type=jnp.float32
    )
    return context.reshape(-1, row_count, head_width)


def shards(
    enc_frames,
    span_counts,
    enc_gain,
    enc_wq,
    enc_wk,
    enc_wv,
    enc_wo,
    adapter,
    owner_map,
    text_embeds,
    llm_gain,
    llm_wq,
    llm_wk,
    llm_wv,
    llm_bq,
    llm_bk,
    llm_bv,
):
    n_tm = lax.axis_size("tm")
    n_t = lax.axis_size("tensor")
    me = lax.axis_index("tm")
    count = FRAMES // POOL
    starts = jnp.cumsum(span_counts) - span_counts
    is_open = jnp.any(starts == me).astype(jnp.int32).reshape(1, 1)
    own = lax.dynamic_slice_in_dim(owner_map, me * count, count, 0)[:, 0]
    order = jnp.arange(count, dtype=jnp.int32)
    earlier = (own[:, None] == own[None, :]) & (order[:, None] < order[None, :])
    ordinal = jnp.sum(earlier.astype(jnp.int32), axis=0)
    target = jnp.pad(own * SLOT + ordinal, (0, POOLED - count), constant_values=-1)[None, :]
    weight = lax.all_gather(
        jnp.concatenate([llm_wq, llm_wk, llm_wv], axis=1), "tm", axis=0, tiled=True
    )
    x4 = run_encoder(
        n_tm, n_t, enc_frames, enc_gain[None, :], enc_wq, enc_wk, enc_wv, enc_wo, target, is_open
    )
    used = SLOT - 1
    filled = (x4[0, :, :used, FEAT] > 0).astype(jnp.int32).reshape(-1)
    pooled = (
        x4[:, :, :used, :FEAT].transpose(1, 2, 0, 3).reshape(n_tm * used, n_t * FEAT)
    )
    adapted = jnp.dot(pooled, adapter, preferred_element_type=jnp.float32).astype(jnp.bfloat16)
    audio = lax.all_gather(adapted, "tensor", axis=1, tiled=True)
    sequence = jnp.concatenate([audio, text_embeds], axis=0)
    row_count = sequence.shape[0]
    row_present = jnp.concatenate([filled, jnp.ones((text_embeds.shape[0],), jnp.int32)])
    positions = jnp.cumsum(row_present) - 1
    seq_normed = root_norm(sequence.astype(jnp.float32), llm_gain).astype(jnp.bfloat16)
    proj = jnp.dot(seq_normed, weight, preferred_element_type=jnp.float32)
    nq = llm_bq.shape[0]
    nk = llm_bk.shape[0]
    query_heads = rotate(
        (proj[:, :nq] + llm_bq).reshape(row_count, -1, LLM_HD).transpose(1, 0, 2), positions
    ).astype(jnp.bfloat16)
    key_heads = rotate(
        (proj[:, nq : nq + nk] + llm_bk).reshape(row_count, -1, LLM_HD).transpose(1, 0, 2),
        positions,
    ).astype(jnp.bfloat16)
    value_heads = (
        (proj[:, nq + nk :] + llm_bv)
        .astype(jnp.bfloat16)
        .reshape(row_count, -1, LLM_HD)
        .transpose(1, 0, 2)
    )
    context_heads = grouped_attention(query_heads, key_heads, value_heads, row_present, positions)
    merged = context_heads.transpose(1, 0, 2).reshape(row_count, -1)
    return (merged * row_present[:, None].astype(jnp.float32)).astype(jnp.bfloat16)


def solution(mesh):
    placed = (
        P("tm", None),
        P(),
        P(),
        P(None, "tensor"),
        P(None, "tensor"),
        P(None, "tensor"),
        P("tensor", None),
        P(None, "tensor"),
        P(),
        P("tm", None),
        P(),
        P("tm", "tensor"),
        P("tm", "tensor"),
        P("tm", "tensor"),
        P("tensor"),
        P("tensor"),
        P("tensor"),
    )
    return jax.shard_map(
        shards, mesh=mesh, in_specs=placed, out_specs=P("tm", "tensor"), check_vma=False
    )
```

profile of v0, /device:TPU:1, one launch (start us, length us, event | category | flops | bytes accessed | tf_op | source)
XLA Modules:
  0.0 277.2 jit_solution(11484671432866891395)
XLA Ops:
  6.5 1.0 reduce-window.20
  7.5 1.3 compare_reduce_fusion.1
  9.5 0.8 dynamic-slice_reduce_fusion
  10.2 0.1 convert_reduce_fusion
  10.4 0.6 broadcast_in_dim.13.target_ref
  11.0 1.3 broadcast_in_dim.12.gain_ref
  12.3 89.3 %shard_map.163 = bf16[4,64,8,384]{3,2,1,0:T(8,128)(2,1)} custom-call(bf16[1500,1280]{1,0:T(8,128)(2,1)} %frames_ref.1, f32[1,1280]{1,0:T(1,128)} %broadcast_in_dim.12.gain_ref, bf16[1280,256]{1,0:T(8,128)(2,1)} %wq_ref.1, bf16[1280,256]{1,0:T(8,128)(2,1)} %wk_ref.1, bf16[1280,256]{1,0:T(8,128)(2,1)} %wv_ref.1, bf16[256,1280]{1,0:T(8,128)(2,1)} %wo_ref.1, ...), custom_call_target="tpu_custom_call" | custom-call | flops 20000000000 | bytes 20000000 | tf_op jit(solution)/shard_map/pallas_call | solution.py:272
  101.6 1.6 slice_bitcast_fusion
  103.2 2.9 %copy.28 = bf16[64,7,4,320]{3,2,1,0:T(4,128)(2,1)} copy(bf16[64,7,4,320]{3,1,0,2:T(8,128)(2,1)S(1)} %slice_bitcast_fusion) | data formatting | bytes 2293760 | tf_op jit(solution)/shard_map/transpose | solution.py:395
  106.0 2.8 %reshape.318 = bf16[448,1280]{1,0:T(8,128)(2,1)S(1)} reshape(bf16[64,7,4,320]{3,2,1,0:T(4,128)(2,1)} %copy.28) | data formatting | bytes 2293760 | tf_op jit(solution)/shard_map/reshape | solution.py:395
  108.9 2.2 convolution_convert_fusion
  111.1 0.3 all-gather.5.cloned.1.call-start
  111.4 1.4 pad_maximum_fusion.2
  112.8 2.1 compare_reduce_fusion
  115.0 0.2 convert_element_type.48
  115.1 0.3 reduce-window.21
  115.8 0.3 fusion.13
  116.1 1.0 multiply_cosine_fusion.1
  117.1 33.3 %all-gather.3.cloned.1.call-done = bf16[448,3584]{1,0:T(8,128)(2,1)} async-done(((bf16[448,896]{1,0:T(8,128)(2,1)}), bf16[448,3584]{1,0:T(8,128)(2,1)}) %all-gather.3.cloned.1.call-update) | async-done | bytes 3211280 | tf_op jit(solution)/shard_map/all_gather | solution.py:398
  150.5 2.9 %fusion.1 = f32[512]{0:T(512)S(1)} fusion(bf16[64,3584]{1,0:T(8,128)(2,1)} %param.26, bf16[448,3584]{1,0:T(8,128)(2,1)} %all-gather.3.cloned.1.call-done), kind=kLoop, calls=%fused_computation.3 | loop fusion | flops 11009536 | bytes 3672064 | tf_op jit(solution)/shard_map/reduce_sum | solution.py:312
  153.3 83.3 %all-gather.5.cloned.1.call-done = bf16[3584,1152]{1,0:T(8,128)(2,1)} async-done(((bf16[56,1152]{1,0:T(8,128)(2,1)}), bf16[3584,1152]{1,0:T(8,128)(2,1)}) %all-gather.5.cloned.1.call-update) | async-done | bytes 8257552 | tf_op jit(solution)/shard_map/all_gather | solution.py:386
  236.6 9.3 %fusion.5 = f32[512,1152]{1,0:T(8,128)S(1)} fusion(bf16[3584,1152]{1,0:T(8,128)(2,1)} %all-gather.5.cloned.1.call-done, f32[3584]{0:T(1024)} %param.27, f32[512]{0:T(512)S(1)} %add_rsqrt_fusion, bf16[64,3584]{1,0:T(8,128)(2,1)S(1)} %copy-done.2, bf16[448,3584]{1,0:T(8,128)(2,1)} %all-gather.3.cloned.1.call-done), kind=kOutput, calls=%fused_computation.10 | convolution fusion | flops 4240703488 | bytes 14303232 | tf_op jit(solution)/shard_map/dot_general | solution.py:404
  246.0 1.2 fusion.35
  247.3 1.4 slice_add_fusion
  248.7 2.8 %copy.29 = f32[512,896]{0,1:T(8,128)} copy(f32[512,896]{1,0:T(8,128)} %slice_add_fusion) | data formatting | bytes 3670016 | tf_op jit(solution)/shard_map/add | solution.py:408
  251.5 2.8 copy.30
  254.3 2.7 subtract_convert_fusion
  257.0 1.2 fusion.14
  258.2 3.4 %fusion.41 = (f32[7,512]{1,0:T(8,128)S(1)}, f32[7,512,512]{1,2,0:T(8,128)S(1)}) fusion(f32[7,512,512]{1,2,0:T(8,128)S(1)} %fusion.14, pred[512,512]{0,1:T(8,128)(4,1)S(1)} %fusion.13), kind=kOutput, calls=%fused_computation.74 | output fusion | flops 11010559 | bytes 14956544 | tf_op jit(solution)/shard_map/sub | solution.py:348
  261.6 3.3 %fusion.11 = f32[7,512,128]{1,2,0:T(8,128)} fusion(f32[7,512,512]{1,2,0:T(8,128)S(1)} %get-tuple-element.17, f32[7,512]{1,0:T(8,128)S(1)} %get-tuple-element.16, f32[512,1152]{1,0:T(8,128)} %copy-done.1, f32[128]{0:T(128)S(1)} %copy-done.8), kind=kOutput, calls=%fused_computation.16 | convolution fusion | flops 473563136 | bytes 9452032 | tf_op jit(solution)/shard_map/kgqs,ksd->kgqd/dot_general | solution.py:350
  265.0 2.8 copy.33
  267.8 2.6 multiply_convert_fusion
  (31 shorter events, 0.7 us)
Async XLA Ops:
  6.5 102.3 %copy-start = (bf16[1280,896]{1,0:T(8,128)(2,1)S(1)}, bf16[1280,896]{1,0:T(8,128)(2,1)}, u32[]{:S(2)}) copy-start(bf16[1280,896]{1,0:T(8,128)(2,1)} %param.24) | copy-start | bytes 6881284
  6.5 143.9 %all-gather.3.cloned.1.call-start = ((), (), s32[]{:S(2)}) async-start(), calls=%async_computation | async-start | bytes 4014080 | tf_op jit(solution)/shard_map/all_gather | solution.py:398
  108.8 2.5 copy-start.3
  111.1 125.5 %copy-start.2 = (bf16[64,3584]{1,0:T(8,128)(2,1)S(1)}, bf16[64,3584]{1,0:T(8,128)(2,1)}, u32[]{:S(2)}) copy-start(bf16[64,3584]{1,0:T(8,128)(2,1)} %param.26) | copy-start | bytes 1376260
  111.1 125.5 %all-gather.5.cloned.1.call-start = ((), (), s32[]{:S(2)}) async-start(), calls=%async_computation.1 | async-start | bytes 8386560 | tf_op jit(solution)/shard_map/all_gather | solution.py:386
  115.6 0.6 copy-start.5
  153.3 94.0 %copy-start.4 = (f32[896]{0:T(1024)S(1)}, f32[896]{0:T(1024)}, u32[]{:S(2)}) copy-start(f32[896]{0:T(1024)} %param.31) | copy-start | bytes 10756
  236.6 9.3 %copy-start.7 = (f32[128]{0:T(128)S(1)}, f32[128]{0:T(128)}, u32[]{:S(2)}) copy-start(f32[128]{0:T(128)} %param.32) | copy-start | bytes 1540
  236.6 9.3 %copy-start.6 = (f32[64]{0:T(128)S(1)}, f32[64]{0:T(128)}, u32[]{:S(2)}) copy-start(f32[64]{0:T(128)} %copy-done.5) | copy-start | bytes 772
  245.9 1.4 copy-start.1
  258.2 3.4 %copy-start.8 = (f32[128]{0:T(128)S(1)}, f32[128]{0:T(128)}, u32[]{:S(2)}) copy-start(f32[128]{0:T(128)} %param.33) | copy-start | bytes 1540
Sparse Core Ops, SparseCore 0:
  111.2 39.1 all-gather.2
  153.1 83.4 all-gather.4
where the time goes:
time: 278 us; the launch traced here: 277 us
  waiting for transfers between devices  117 us (42%)
  Pallas kernels  89.3 us (32%)
  other arithmetic  21.9 us (8%)
  local copies, waits for them, and re-layouts  18.8 us (7%)
  matrix products  16.1 us (6%)
  between operations  14.2 us (5%)
    pallas_call x1, Pallas kernels, run_encoder(): pl.pallas_call(functools.partial(encoder_kernel, n_tm, n_t), out_shape=ja...  89.3 us
    all_gather x1, waiting for transfers between devices, shards(): lax.all_gather(jnp.concatenate([llm_wq, llm_wk, llm_wv], axis=1), 'tm', a...  83.3 us
    all_gather x1, waiting for transfers between devices, shards(): audio = lax.all_gather(adapted, 'tensor', axis=1, tiled=True)  33.3 us
    dot_general x1, matrix products, shards(): proj = jnp.dot(seq_normed, weight, preferred_element_type=jnp.float32)  9.29 us
  transfers between devices with their start and end apart: 2, of which 2 were waited for; matrix products, arithmetic and copies ran while one was open for 3% of the time, Pallas kernels for 0%

commit v1 on v0

v1 whole, which is shorter than its diff:
```python
import functools
import math
import types

import jax
import jax.numpy as jnp
import numpy as np
from jax import lax
from jax.experimental import pallas as pl
from jax.experimental.pallas import tpu as pltpu
from jax.sharding import PartitionSpec as P

B16 = jnp.bfloat16
F32 = jnp.float32
MESH = pl.DeviceIdType.MESH

ENC_HD = 64
FRAMES = 1500
POOL = 4
LLM_HD = 128
PAD = 1536
ROWS = 384
TILES = PAD // ROWS
PROWS = ROWS // POOL
PART = PAD // 2
POOLED = PAD // POOL
SLOT = 8
FEAT = 320
WIDE = 384
LOG2E = math.log2(math.e)
NX = 4
NZ = 8
NC = 2
D_LLM = 3584
SEQ = 512
CHUNK = 56
PIECE = NC * CHUNK
BLOCK = 256
AROWS = 80
QKV = 1152


def dot(a, b):
    return jnp.dot(a, b, preferred_element_type=F32)


INPUTS = ("frames", "wq", "wk", "wv", "adapter", "wo", "text", "rope")
SMALL = ("gain", "owners", "counts", "llm_gain", "pq", "pk", "pv", "bq", "bk", "bv")
HBM, SEND, RECV = "hbm_", "_send", "_recv"
GROUPS = 4


def block_kernel(n_tm, n_t, names, *refs):
    r = types.SimpleNamespace(**dict(zip(names, refs, strict=True)))
    me = lax.axis_index("tm")
    t = lax.axis_index("tensor")
    z = me // (NX * NC)
    xx = lax.rem(me // NC, NX)
    c = lax.rem(me, NC)
    lane = lax.broadcasted_iota(jnp.int32, (1, 256), 1) // ENC_HD
    heads = 256 // ENC_HD

    def at(zz, xv, cv):
        return ((zz * NX + xv) * NC + cv, t)

    def x_other(k):
        return lax.rem(xx + k, NX)

    def t_other(k):
        return lax.rem(t + k, n_t)

    mate = at(z, xx, 1 - c)

    def remote(src, dst, send, recv, to):
        return pltpu.make_async_remote_copy(
            src_ref=src, dst_ref=dst, send_sem=send, recv_sem=recv, device_id=to, device_id_type=MESH
        )

    def drain(ref, sem):
        pltpu.make_async_copy(ref, ref, sem).wait()

    barrier = pltpu.get_barrier_semaphore()

    def greet(k, _):
        pl.semaphore_signal(
            barrier, inc=1, device_id=(lax.rem(me + k, n_tm), t), device_id_type=MESH
        )
        return 0

    lax.fori_loop(1, n_tm, greet, 0)
    for k in range(1, n_t):
        pl.semaphore_signal(barrier, inc=1, device_id=(me, t_other(k)), device_id_type=MESH)

    def fetched(name):
        return pltpu.make_async_copy(
            getattr(r, HBM + name), getattr(r, name), r.in_sem.at[INPUTS.index(name)]
        )

    for name in INPUTS:
        fetched(name).start()

    cut = 640

    def ring(k):
        return lax.rem(z + NZ + k, NZ)

    def ring_sent(buf, sems, k, to, step, cols=None):
        ref = buf.at[c, ring(k)]
        if cols is not None:
            ref = buf.at[c, ring(k), :, cols]
        remote(
            ref, ref, getattr(r, sems + SEND), getattr(r, sems + RECV).at[step], at(ring(to), xx, c)
        ).start()

    def to_mate(buf, sems, k):
        ref = buf.at[c, ring(k)]
        remote(ref, ref, getattr(r, sems + SEND), getattr(r, sems + RECV), mate).start()

    def ring_first(buf, sems):
        for k in (2, -2, 1, -1):
            ring_sent(buf, sems, 0, k, 0)

    def ring_second(buf, sems, mate_sems):
        drain(buf.at[c, pl.ds(0, 4)], getattr(r, sems + RECV).at[0])
        ring_sent(buf, sems, -2, 2, 1, slice(0, cut))
        ring_sent(buf, sems, 2, -2, 1, slice(cut, QKV))
        ring_sent(buf, sems, -2, 1, 1)
        ring_sent(buf, sems, 2, -1, 1)
        for k in (0, 1, -1, 2, -2):
            to_mate(buf, mate_sems, k)

    def ring_last(buf, sems, mate_sems):
        drain(buf.at[c, pl.ds(0, 3)], getattr(r, sems + RECV).at[1])
        for k in (3, -3, 4):
            to_mate(buf, mate_sems, k)

    def ring_done(buf, sems, mate_sems):
        drain(buf.at[c, pl.ds(0, NZ - 1)], getattr(r, sems + SEND))
        drain(buf.at[c], getattr(r, mate_sems + SEND))
        drain(buf.at[1 - c], getattr(r, mate_sems + RECV))

    nq, nk = r.pq.shape[1], r.pk.shape[1]
    own_w = r.wz.at[c, z]
    own_w[:, :nq] = r.pq[...]
    own_w[:, nq : nq + nk] = r.pk[...]
    own_w[:, nq + nk :] = r.pv[...]

    def adapter_rows(k):
        return remote(
            r.asel.at[xx],
            r.arow.at[t],
            r.as_send.at[k - 1],
            r.as_recv.at[k - 1],
            (me, t_other(k)),
        )

    def text_rows(k):
        xv = x_other(k)
        return remote(
            r.tp.at[xv],
            r.trow.at[xx],
            r.tp_send.at[k - 1],
            r.tp_recv.at[k - 1],
            at(z, xv, c),
        )

    for name in ("frames", "wq", "wk", "wv"):
        fetched(name).wait()
    tail_ref, frames_ref = r.tail, r.frames
    gain = r.gain[...].reshape(1, -1)
    tail_ref[...] = jnp.zeros_like(tail_ref)
    tail_ref[0 : FRAMES - 1280, :] = frames_ref[1280:FRAMES, :]
    prow = lax.broadcasted_iota(jnp.int32, (64, 256), 0)
    pcol = lax.broadcasted_iota(jnp.int32, (64, 256), 1)
    pool = jnp.where(pcol // POOL == prow, 0.25, 0.0).astype(B16)

    def project(raw, i):
        rows = pl.ds(pl.multiple_of(i * 256, 256), 256)
        x = raw.astype(F32)
        mean = jnp.mean(x, axis=-1, keepdims=True)
        cent = x - mean
        var = jnp.mean(cent * cent, axis=-1, keepdims=True)
        normed = (cent * lax.rsqrt(var + 1e-05) * gain).astype(B16)
        r.q[rows, :] = (dot(normed, r.wq[...]) * (ENC_HD**-0.5 * LOG2E)).astype(B16)
        r.kt[:, rows] = jnp.transpose(dot(normed, r.wk[...])).astype(B16)
        r.v[rows, :] = dot(normed, r.wv[...]).astype(B16)
        res = dot(pool, raw)
        prows = pl.ds(pl.multiple_of(i * 64, 64), 64)
        for tt in range(n_t):

            @pl.when(t == tt)
            def _():
                r.res[prows, :] = res[:, tt * FEAT : (tt + 1) * FEAT]

    def project_block(i, _):
        project(frames_ref[pl.ds(pl.multiple_of(i * 256, 256), 256), :], i)
        return 0

    lax.fori_loop(0, 5, project_block, 0)
    project(tail_ref[...], 5)

    pl.semaphore_wait(barrier, n_tm - 1 + n_t - 1)
    ring_first(r.wz, "wz")

    onward = (lax.rem(me + 1, n_tm), t)

    def keys_on(part):
        cols = slice(part * PART, (part + 1) * PART)
        i = 2 * part
        return (
            remote(r.kt.at[:, cols], r.ktp.at[:, cols], r.kv_send.at[i], r.kv_recv.at[i], onward),
            remote(r.v.at[cols], r.vp.at[cols], r.kv_send.at[i + 1], r.kv_recv.at[i + 1], onward),
        )

    for part in range(2):
        for copy in keys_on(part):
            copy.start()

    fetched("adapter").wait()
    width = r.adapter.shape[1]
    llm_gain = r.llm_gain[...].reshape(1, -1)
    r.asel[...] = jnp.zeros_like(r.asel)
    r.gp[...] = jnp.zeros_like(r.gp)
    own_a = r.adapter[pl.ds(pl.multiple_of((c * NZ + z) * AROWS, AROWS), AROWS), :]
    for xv in range(NX):
        for zz in range(2):
            lo = zz * NX * PIECE + xv * PIECE
            r.asel[xv, :, zz * PIECE : (zz + 1) * PIECE] = own_a[:, lo : lo + PIECE]
            for tt in range(n_t):
                to = tt * BLOCK + zz * PIECE
                r.gp[xv, 0:1, to : to + PIECE] = llm_gain[:, tt * width + lo : tt * width + lo + PIECE]
    r.arow[t] = r.asel[xx]
    for k in range(1, n_t):
        adapter_rows(k).start()

    tail_lane = lax.broadcasted_iota(jnp.int32, (1, 128), 1) < FRAMES - (PAD - 128)

    def head_masks(values_ref, lo, size):
        for h in range(heads):
            r.vm[h, lo : lo + size] = jnp.where(
                lane == h, values_ref[lo : lo + size, :], jnp.ones((), B16)
            )

    def attend(rows, keys_ref, lo, size):
        q = r.q[rows, :]
        out = jnp.zeros((ROWS, 256), F32)
        top = jnp.zeros((ROWS, 256), F32)
        den = jnp.zeros((ROWS, 256), F32)
        for h in range(heads):
            s = dot(jnp.where(lane == h, q, jnp.zeros_like(q)), keys_ref[:, lo : lo + size])
            if lo + size == PAD:
                end = jnp.where(tail_lane, s[:, size - 128 :], -1e30)
                s = jnp.concatenate([s[:, : size - 128], end], axis=1)
            m = jnp.max(s, axis=1, keepdims=True)
            p = jnp.exp2(s - m).astype(B16)
            o = dot(p, r.vm[h, lo : lo + size])
            col = 255 if h < heads - 1 else 0
            out = jnp.where(lane == h, o, out)
            top = jnp.where(lane == h, m, top)
            den = jnp.where(lane == h, o[:, col : col + 1], den)
        return out, top, den

    head_masks(r.v, 0, PAD)

    def own_half(i, _):
        @pl.when(i == TILES - 1)
        def _():
            ring_second(r.wz, "wz", "wm")

        rows = pl.ds(pl.multiple_of(i * ROWS, ROWS), ROWS)
        out, top, den = attend(rows, r.kt, 0, PAD)
        r.o1[rows, :] = out
        r.m1[rows, :] = top
        r.l1[rows, :] = den
        return 0

    lax.fori_loop(0, TILES, own_half, 0)

    fetched("text").wait()
    text = r.text[...].astype(F32)
    power = jnp.mean(text * text, axis=-1, keepdims=True)
    text = (text * lax.rsqrt(power + 1e-06) * llm_gain).astype(B16)
    r.tp[...] = jnp.zeros_like(r.tp)
    for xv in range(NX):
        for tt in range(n_t):
            for zz in range(2):
                lo = tt * width + zz * NX * PIECE + xv * PIECE
                to = tt * BLOCK + zz * PIECE
                r.tp[xv, :, to : to + PIECE] = text[:, lo : lo + PIECE]
    r.trow[xx] = r.tp[xx]
    def fused_sent(k):
        return remote(
            r.fx.at[xx],
            r.fx.at[xx],
            r.fx_send.at[k - 1],
            r.fx_recv.at[k - 1],
            at(z, x_other(k), c),
        )

    def text_sent(k):
        xv = x_other(k)
        return remote(
            r.tsend.at[xv],
            r.trecv.at[xx],
            r.tx_send.at[k - 1],
            r.tx_recv.at[k - 1],
            at(z, xv, c),
        )

    def multiply_slab():
        ring_done(r.wz, "wz", "wm")
        for k in range(1, n_t):
            adapter_rows(k).wait()
        for tt in range(n_t):
            rows = [
                r.wz[cv, 2 * tt + zz].astype(F32) for zz in range(2) for cv in range(NC)
            ]
            rows.append(jnp.zeros((BLOCK - 2 * PIECE, QKV), F32))
            r.wslab[tt * BLOCK : (tt + 1) * BLOCK, :] = jnp.concatenate(rows, axis=0).astype(B16)
        fused = jnp.zeros((AROWS, QKV), F32)
        gains = r.gp[xx]
        for tt in range(n_t):
            cols = slice(tt * BLOCK, (tt + 1) * BLOCK)
            scaled = (r.arow[tt].astype(F32) * gains[0:1, cols]).astype(B16)
            fused = fused + dot(scaled, r.wslab[cols, :])
        r.fx[xx] = fused.astype(B16)
        for k in range(1, NX):
            fused_sent(k).start()

    def multiply_text():
        for k in range(1, NX):
            text_rows(k).wait()
        for xv in range(NX):
            r.tsend[xv] = dot(r.trow[xv], r.wslab[...]).astype(B16)
        r.trecv[xx] = r.tsend[xx]
        for k in range(1, NX):
            text_sent(k).start()

    def spread_fused():
        for k in range(1, NX):
            fused_sent(k).wait()
        total = r.fx[0].astype(F32)
        for xv in range(1, NX):
            total = total + r.fx[xv].astype(F32)
        r.fall[c, z] = total.astype(B16)
        ring_first(r.fall, "fz")
        for k in range(1, NX):
            text_rows(k).start()

    for copy in keys_on(0):
        copy.wait()
    head_masks(r.vp, 0, PART)
    fetched("wo").wait()
    begin = jnp.int32(0)
    openings = jnp.int32(0)
    for i in range(r.counts.shape[0]):
        openings = openings + jnp.where(begin == me, 1, 0)
        begin = begin + r.counts[i]
    is_open = openings > 0
    trow = lax.broadcasted_iota(jnp.int32, (PROWS, ROWS), 0)
    tcol = lax.broadcasted_iota(jnp.int32, (PROWS, ROWS), 1)
    tile_pool = jnp.where(tcol // POOL == trow, 0.25, 0.0).astype(B16)

    def summed(i, k):
        rows = pl.ds(pl.multiple_of(i * PROWS, PROWS), PROWS)
        to = t_other(k)
        return remote(
            r.part.at[to, rows],
            r.rs.at[t, rows],
            r.rs_send.at[i, k - 1],
            r.rs_recv.at[i, k - 1],
            (me, to),
        )

    def merged(rows, lo):
        out, top, den = attend(rows, r.ktp, lo, PART)
        m1 = r.m1[rows, :]
        both = jnp.where(is_open, m1, jnp.maximum(m1, top))
        w1 = jnp.exp2(m1 - both)
        w2 = jnp.where(is_open, 0.0, jnp.exp2(jnp.minimum(top - both, 0.0)))
        return w1 * r.o1[rows, :] + w2 * out, both, w1 * r.l1[rows, :] + w2 * den

    def prior_first(i, _):
        @pl.when(i == 1)
        def _():
            ring_last(r.wz, "wz", "wm")

        @pl.when(i == TILES - 1)
        def _():
            multiply_slab()

        rows = pl.ds(pl.multiple_of(i * ROWS, ROWS), ROWS)
        out, top, den = merged(rows, 0)
        r.o1[rows, :] = out
        r.m1[rows, :] = top
        r.l1[rows, :] = den
        return 0

    lax.fori_loop(0, TILES, prior_first, 0)

    for copy in keys_on(1):
        copy.wait()
    head_masks(r.vp, PART, PART)

    def prior_second(i, _):
        @pl.when(i == TILES - 1)
        def _():
            spread_fused()

        rows = pl.ds(pl.multiple_of(i * ROWS, ROWS), ROWS)
        out, top, den = merged(rows, PART)
        ctx = (out / den).astype(B16)
        pooled = dot(tile_pool, ctx).astype(B16)
        partial = dot(pooled, r.wo[...]).astype(B16)
        prows = pl.ds(pl.multiple_of(i * PROWS, PROWS), PROWS)
        for tt in range(n_t):
            r.part[tt, prows, :] = partial[:, tt * FEAT : (tt + 1) * FEAT]
        for k in range(1, n_t):
            summed(i, k).start()
        return 0

    lax.fori_loop(0, TILES, prior_second, 0)

    def summed_wait(i, _):
        for k in range(1, n_t):
            summed(i, k).wait()
        return 0

    lax.fori_loop(0, TILES, summed_wait, 0)

    total = r.part[t].astype(F32)
    for k in range(1, n_t):
        total = total + r.rs[t_other(k)].astype(F32)
    pooled = (r.res[...] + total).astype(B16)
    wide = jnp.concatenate([pooled, jnp.ones((POOLED, WIDE - FEAT), B16)], axis=1)
    owners = jnp.broadcast_to(r.owners[...].astype(F32), (128, POOLED))
    same = jnp.transpose(owners)[:, 0:1] == owners[0:1, :]
    first = lax.broadcasted_iota(jnp.int32, (POOLED, POOLED), 0)
    then = lax.broadcasted_iota(jnp.int32, (POOLED, POOLED), 1)
    ordinal = jnp.sum(jnp.where(same & (first < then), 1.0, 0.0), axis=0, keepdims=True)
    target = owners[0:1, :] * SLOT + ordinal
    slot_row = lax.broadcasted_iota(jnp.int32, (n_tm * SLOT, POOLED), 0)
    place = jnp.where(slot_row.astype(F32) == target, 1.0, 0.0).astype(B16)
    slots_ref, x_ref = r.slots, r.x
    slots_ref[...] = dot(place, wide).reshape(n_tm, SLOT, WIDE).astype(B16)
    x_ref[t, 0] = slots_ref[me]
    members = n_tm // GROUPS

    for g in range(GROUPS):

        def routed_start(k, _, g=g):
            to = lax.rem(me + k, n_tm)
            remote(
                slots_ref.at[to], x_ref.at[t, k], r.a2a_send, r.a2a_recv.at[g], (to, t)
            ).start()
            return 0

        lax.fori_loop(max(1, g * members), (g + 1) * members, routed_start, 0)

    multiply_text()

    def handed(g, k):
        rows = pl.ds(g * members, members)
        ref = x_ref.at[t, rows]
        i = (k + 1) // 2
        return remote(
            ref, ref, r.ag_send.at[g, i], r.ag_recv.at[g, i], (me, lax.rem(t + n_t + k, n_t))
        )

    def relayed(g, k):
        part = members // 2
        rows = pl.ds(g * members + (0 if k > 0 else part), part)
        ref = x_ref.at[lax.rem(t + n_t - k, n_t), rows]
        i = (k + 1) // 2
        return remote(
            ref, ref, r.ar_send.at[g, i], r.ar_recv.at[g, i], (me, lax.rem(t + n_t + k, n_t))
        )

    def relay(g):
        for k in (1, -1):
            handed(g, k).wait()
        for k in (1, -1):
            relayed(g, k).start()

    for g in range(GROUPS):
        start = max(1, g * members)
        drain(x_ref.at[t, pl.ds(start, (g + 1) * members - start)], r.a2a_recv.at[g])
        for k in (1, -1):
            handed(g, k).start()
        if g == 1:
            ring_second(r.fall, "fz", "fm")
        if g > 0:
            relay(g - 1)
    relay(GROUPS - 1)
    drain(slots_ref.at[pl.ds(0, n_tm - 1)], r.a2a_send)
    for k in range(1, NX):
        text_sent(k).wait()
    for g in range(GROUPS):
        for k in (1, -1):
            relayed(g, k).wait()

    used = SLOT - 1
    audio = n_tm * used
    fetched("rope").wait()
    srow = lax.broadcasted_iota(jnp.int32, (audio, n_tm * SLOT), 0)
    scol = lax.broadcasted_iota(jnp.int32, (audio, n_tm * SLOT), 1)
    source = (me - (scol >> 3)) & (n_tm - 1)
    place = source * used + (scol & (SLOT - 1))
    compact = jnp.where((place == srow) & ((scol & (SLOT - 1)) < used), 1.0, 0.0).astype(B16)
    flags = None
    for tt in range(n_t):
        rows = x_ref[tt].astype(F32).reshape(n_tm * SLOT, WIDE).astype(B16)
        rows = dot(compact, rows)
        r.xc[:, tt * FEAT : (tt + 1) * FEAT] = rows[:, :FEAT].astype(B16)
        if tt == 0:
            flags = rows[:, FEAT : FEAT + 1]

    adapted = dot(r.xc[...], r.adapter[...])
    power = jnp.sum(adapted * adapted, axis=1, keepdims=True)
    power = jnp.concatenate([power, jnp.zeros((SEQ - audio, 1), F32)], axis=0)
    power = jnp.transpose(jnp.broadcast_to(power, (SEQ, 128)))
    r.ss[t] = power[0:8, :]

    def power_sent(k):
        return remote(
            r.ss.at[t], r.ss.at[t], r.ss_send.at[k - 1], r.ss_recv.at[k - 1], (me, t_other(k))
        )

    for k in range(1, n_t):
        power_sent(k).start()

    present = jnp.concatenate([flags, jnp.ones((SEQ - audio, 1), F32)], axis=0)
    present = jnp.broadcast_to(present, (SEQ, 128))
    row = lax.broadcasted_iota(jnp.int32, (SEQ, SEQ), 0)
    col = lax.broadcasted_iota(jnp.int32, (SEQ, SEQ), 1)
    until = jnp.where(col <= row, 1.0, 0.0).astype(B16)
    position = dot(until, present.astype(B16)) - 1.0
    chosen = jnp.where(col.astype(F32) == position[:, 0:1], 1.0, 0.0).astype(B16)
    high = r.rope[...].astype(B16)
    table = dot(chosen, high) + dot(chosen, (r.rope[...] - high.astype(F32)).astype(B16))
    cosine, sine = table[:, :LLM_HD], table[:, LLM_HD:]
    key_there = jnp.transpose(present)[0:1, :] > 0.5
    r.mask[...] = jnp.where(((col <= row) & key_there) | (col == row), 0.0, -1e30)

    ring_last(r.fall, "fz", "fm")
    ring_done(r.fall, "fz", "fm")
    r.qkv[0:audio, :] = dot(r.xc[...], r.fall[...].reshape(NC * NZ * AROWS, QKV))
    text_part = r.trecv[0].astype(F32)
    for xv in range(1, NX):
        text_part = text_part + r.trecv[xv].astype(F32)
    r.qkv[audio:SEQ, :] = text_part

    for k in range(1, n_t):
        power_sent(k).wait()
    power = r.ss[0]
    for tt in range(1, n_t):
        power = power + r.ss[tt]
    power = jnp.transpose(jnp.broadcast_to(power[0:1, :], (128, SEQ)))
    scale = lax.rsqrt(power * (1.0 / D_LLM) + 1e-06)
    row_of = lax.broadcasted_iota(jnp.int32, (SEQ, 128), 0)
    scale = jnp.where(row_of < audio, scale, 1.0)

    q_bias = r.bq[...].reshape(1, -1)

    def columns(i, bias):
        cols = slice(i * LLM_HD, (i + 1) * LLM_HD)
        return r.qkv[:, cols] * scale + bias

    def rotated(x):
        return x * cosine + pltpu.roll(x, LLM_HD // 2, 1) * sine

    q_heads = nq // LLM_HD
    keys = jnp.transpose(rotated(columns(q_heads, r.bk[...].reshape(1, -1)))).astype(B16)
    values = columns(q_heads + 1, r.bv[...].reshape(1, -1)).astype(B16)
    values = jnp.concatenate([values, jnp.ones((SEQ, LLM_HD), B16)], axis=1)
    for h in range(q_heads):
        bias = q_bias[:, h * LLM_HD : (h + 1) * LLM_HD]
        query = (rotated(columns(h, bias)) * (LLM_HD**-0.5 * LOG2E)).astype(B16)
        for lo in range(0, SEQ, 256):
            rows, end = slice(lo, lo + 256), lo + 256
            s = dot(query[rows], keys[:, :end]) + r.mask[rows, :end]
            m = jnp.max(s, axis=1, keepdims=True)
            o = dot(jnp.exp2(s - m).astype(B16), values[:end])
            ctx = o[:, :LLM_HD] / o[:, LLM_HD:] * present[rows]
            r.out[rows, h * LLM_HD : (h + 1) * LLM_HD] = ctx.astype(B16)


def rope_table():
    half = LLM_HD // 2
    freq = np.exp(
        np.arange(half, dtype=np.float32) * np.float32(-2.0 * math.log(1000000.0) / LLM_HD)
    ).astype(np.float32)
    angles = np.arange(SEQ, dtype=np.float32)[:, None] * freq[None, :]
    cosine = np.cos(angles.astype(np.float64)).astype(np.float32)
    sine = np.sin(angles.astype(np.float64)).astype(np.float32)
    return np.concatenate([cosine, cosine, -sine, sine], axis=1)


def run_block(n_tm, n_t, *args):
    vmem = pl.BlockSpec(memory_space=pltpu.VMEM)
    smem = pl.BlockSpec(memory_space=pltpu.SMEM)
    dma = pltpu.SemaphoreType.DMA
    audio = n_tm * (SLOT - 1)
    scratch = dict(
        tail=((256, 1280), B16),
        q=((PAD, 256), B16),
        kt=((256, PAD), B16),
        v=((PAD, 256), B16),
        ktp=((256, PAD), B16),
        vp=((PAD, 256), B16),
        vm=((256 // ENC_HD, PAD, 256), B16),
        o1=((PAD, 256), F32),
        m1=((PAD, 256), F32),
        l1=((PAD, 256), F32),
        res=((POOLED, FEAT), F32),
        part=((n_t, POOLED, FEAT), B16),
        rs=((n_t, POOLED, FEAT), B16),
        slots=((n_tm, SLOT, WIDE), B16),
        x=((n_t, n_tm, SLOT, WIDE), B16),
        wz=((NC, NZ, CHUNK, QKV), B16),
        wslab=((n_t * BLOCK, QKV), B16),
        tp=((NX, SEQ - audio, n_t * BLOCK), B16),
        gp=((NX, 8, n_t * BLOCK), F32),
        asel=((NX, AROWS, BLOCK), B16),
        arow=((n_t, AROWS, BLOCK), B16),
        trow=((NX, SEQ - audio, n_t * BLOCK), B16),
        tsend=((NX, SEQ - audio, QKV), B16),
        trecv=((NX, SEQ - audio, QKV), B16),
        fx=((NX, AROWS, QKV), B16),
        fall=((NC, NZ, AROWS, QKV), B16),
        xc=((audio, n_t * FEAT), B16),
        ss=((n_t, 8, SEQ), F32),
        qkv=((SEQ, QKV), F32),
        mask=((SEQ, SEQ), F32),
    )
    sems = dict(
        in_sem=(len(INPUTS),),
        kv_send=(4,),
        kv_recv=(4,),
        rs_send=(TILES, n_t - 1),
        rs_recv=(TILES, n_t - 1),
        a2a_send=(),
        a2a_recv=(GROUPS,),
        ag_send=(GROUPS, 2),
        ag_recv=(GROUPS, 2),
        ar_send=(GROUPS, 2),
        ar_recv=(GROUPS, 2),
        wz_send=(),
        wz_recv=(2,),
        wm_send=(),
        wm_recv=(),
        as_send=(n_t - 1,),
        as_recv=(n_t - 1,),
        tp_send=(NX - 1,),
        tp_recv=(NX - 1,),
        fx_send=(NX - 1,),
        fx_recv=(NX - 1,),
        tx_send=(NX - 1,),
        tx_recv=(NX - 1,),
        fz_send=(),
        fz_recv=(2,),
        fm_send=(),
        fm_recv=(),
        ss_send=(n_t - 1,),
        ss_recv=(n_t - 1,),
    )
    held = {n: (a.shape, a.dtype) for n, a in zip(INPUTS, args, strict=False)} | scratch
    shapes = [pltpu.VMEM(*a) for a in held.values()]
    shapes += [dma(a) if a else dma for a in sems.values()]
    names = [HBM + n for n in INPUTS] + [*SMALL, "out", *held, *sems]
    return pl.pallas_call(
        functools.partial(block_kernel, n_tm, n_t, names),
        out_shape=jax.ShapeDtypeStruct((SEQ, args[len(INPUTS) + SMALL.index("pq")].shape[1]), B16),
        in_specs=[pl.BlockSpec(memory_space=pl.ANY)] * len(INPUTS)
        + [smem if n == "counts" else vmem for n in SMALL],
        out_specs=vmem,
        scratch_shapes=shapes,
        compiler_params=pltpu.CompilerParams(
            collective_id=0, has_side_effects=True, vmem_limit_bytes=62 << 20
        ),
        cost_estimate=pl.CostEstimate(
            flops=20_000_000_000, bytes_accessed=20_000_000, transcendentals=20_000_000
        ),
    )(*args)


def shards(
    enc_frames,
    span_counts,
    enc_gain,
    enc_wq,
    enc_wk,
    enc_wv,
    enc_wo,
    adapter,
    owner_map,
    text_embeds,
    llm_gain,
    llm_wq,
    llm_wk,
    llm_wv,
    llm_bq,
    llm_bk,
    llm_bv,
):
    n_tm = lax.axis_size("tm")
    n_t = lax.axis_size("tensor")
    me = lax.axis_index("tm")
    count = FRAMES // POOL
    owners = lax.dynamic_slice_in_dim(owner_map, me * count, count, 0)[:, 0]
    owners = jnp.pad(owners, (0, POOLED - count), constant_values=-n_tm)[None, :]
    return run_block(
        n_tm,
        n_t,
        enc_frames,
        enc_wq,
        enc_wk,
        enc_wv,
        adapter,
        enc_wo,
        text_embeds,
        jnp.asarray(rope_table()),
        enc_gain,
        owners,
        span_counts,
        llm_gain,
        llm_wq,
        llm_wk,
        llm_wv,
        llm_bq,
        llm_bk,
        llm_bv,
    )


def solution(mesh):
    placed = (
        P("tm", None),
        P(),
        P(),
        P(None, "tensor"),
        P(None, "tensor"),
        P(None, "tensor"),
        P("tensor", None),
        P(None, "tensor"),
        P(),
        P("tm", None),
        P(),
        P("tm", "tensor"),
        P("tm", "tensor"),
        P("tm", "tensor"),
        P("tensor"),
        P("tensor"),
        P("tensor"),
    )
    return jax.shard_map(
        shards, mesh=mesh, in_specs=placed, out_specs=P("tm", "tensor"), check_vma=False
    )
```

time: 278 us -> 121 us (0.44)
  waiting for transfers between devices: 117 us -> 0 us
  Pallas kernels: 89.3 us -> 117 us
  other arithmetic: 21.9 us -> 0 us
  matrix products: 16.1 us -> 0 us
  local copies, waits for them, and re-layouts: 18.8 us -> 3.73 us
  between operations: 14.2 us -> 0.02 us
    all_gather x2 -> x0, waiting for transfers between devices: 117 us -> none  [the longest x1 83.3 us: shards(): lax.all_gather(jnp.concatenate([llm_wq, llm_wk, llm_wv], axis=1), 'tm', a...]
    pallas_call x1, Pallas kernels: 89.3 us -> 117 us  [run_block(): pl.pallas_call(functools.partial(block_kernel, n_tm, n_t, names), out_sha...]
    dot_general x4 -> x0, matrix products: 16.1 us -> none  [the longest x1 9.29 us: shards(): proj = jnp.dot(seq_normed, weight, preferred_element_type=jnp.float32)]
    reshape x3 -> x0, local copies, waits for them, and re-layouts: 8.3 us -> none  [the longest x1 2.78 us: shards(): x4[:, :, :used, :FEAT].transpose(1, 2, 0, 3)]
    transpose x2 -> x0, local copies, waits for them, and re-layouts: 4.42 us -> none  [shards(): x4[:, :, :used, :FEAT].transpose(1, 2, 0, 3)]
    another operation x5 -> x0, other arithmetic: 4.06 us -> none
    sub x1 -> x0, other arithmetic: 3.4 us -> none  [grouped_attention(): weights = jnp.exp(scores - peak)]
    reduce_sum x2 -> x0, other arithmetic: 3 us -> none  [the longest x1 2.85 us: root_norm(): power = jnp.mean(samples * samples, axis=-1, keepdims=True)]
  transfers between devices with their start and end apart: 2 -> 0, of which waited for: 2 -> 0; matrix products, arithmetic and copies ran while one was open for 3% -> 0% of each run, Pallas kernels for 0% -> 0%
where the time goes in v1:
time: 121 us; the launch traced here: 120 us
  Pallas kernels  117 us (97%)
  local copies, waits for them, and re-layouts  3.73 us (3%)
    pallas_call x1, Pallas kernels, run_block(): pl.pallas_call(functools.partial(block_kernel, n_tm, n_t, names), out_sha...  117 us
    unnamed x3, local copies, waits for them, and re-layouts  3.07 us

profile of v1, /device:TPU:1, one launch (start us, length us, event | category | flops | bytes accessed | tf_op | source)
XLA Modules:
  0.0 120.5 jit_solution(4186637020866043538)
XLA Ops:
  0.0 0.0 copy-start
  0.0 0.9 copy-done
  0.9 0.1 dynamic-slice_reduce_fusion
  1.0 0.6 broadcast_in_dim.3.refs_9_
  1.6 116.7 %shard_map.172 = bf16[512,896]{1,0:T(8,128)(2,1)} custom-call(bf16[1500,1280]{1,0:T(8,128)(2,1)} %refs_0_.1, bf16[1280,256]{1,0:T(8,128)(2,1)} %refs_1_.1, bf16[1280,256]{1,0:T(8,128)(2,1)} %refs_2_.1, bf16[1280,256]{1,0:T(8,128)(2,1)} %refs_3_.1, bf16[1280,896]{1,0:T(8,128)(2,1)} %refs_4_.1, bf16[256,1280]{1,0:T(8,128)(2,1)} %refs_5_.1, ...), custom_call_target="tpu_custom_call" | custom-call | flops 20000000000 | bytes 20000000 | tf_op jit(solution)/shard_map/pallas_call | solution.py:671
  118.3 2.2 %copy.20 = bf16[512,896]{1,0:T(8,128)(2,1)} copy(bf16[512,896]{1,0:T(8,128)(2,1)} %shard_map.172) | data formatting | bytes 1835008
  (1 shorter events, 0.0 us)
Async XLA Ops:
  0.0 0.9 copy-start

commit v2 on v1

--- a/solution.py
+++ b/solution.py
@@ -196,11 +196,11 @@
         project(frames_ref[pl.ds(pl.multiple_of(i * 256, 256), 256), :], i)
         return 0
 
-    lax.fori_loop(0, 5, project_block, 0)
-    project(tail_ref[...], 5)
-
+    lax.fori_loop(0, 2, project_block, 0)
     pl.semaphore_wait(barrier, n_tm - 1 + n_t - 1)
     ring_first(r.wz, "wz")
+    lax.fori_loop(2, 5, project_block, 0)
+    project(tail_ref[...], 5)
 
     onward = (lax.rem(me + 1, n_tm), t)
 
@@ -263,7 +263,7 @@
     head_masks(r.v, 0, PAD)
 
     def own_half(i, _):
-        @pl.when(i == TILES - 1)
+        @pl.when(i == 2)
         def _():
             ring_second(r.wz, "wz", "wm")
 
@@ -288,6 +288,7 @@
                 to = tt * BLOCK + zz * PIECE
                 r.tp[xv, :, to : to + PIECE] = text[:, lo : lo + PIECE]
     r.trow[xx] = r.tp[xx]
+    ring_last(r.wz, "wz", "wm")
     def fused_sent(k):
         return remote(
             r.fx.at[xx],
@@ -372,8 +373,8 @@
             (me, to),
         )
 
-    def merged(rows, lo):
-        out, top, den = attend(rows, r.ktp, lo, PART)
+    def merged(rows, lo, size):
+        out, top, den = attend(rows, r.ktp, lo, size)
         m1 = r.m1[rows, :]
         both = jnp.where(is_open, m1, jnp.maximum(m1, top))
         w1 = jnp.exp2(m1 - both)
@@ -381,34 +382,21 @@
         return w1 * r.o1[rows, :] + w2 * out, both, w1 * r.l1[rows, :] + w2 * den
 
     def prior_first(i, _):
-        @pl.when(i == 1)
-        def _():
-            ring_last(r.wz, "wz", "wm")
-
-        @pl.when(i == TILES - 1)
-        def _():
-            multiply_slab()
-
         rows = pl.ds(pl.multiple_of(i * ROWS, ROWS), ROWS)
-        out, top, den = merged(rows, 0)
+        out, top, den = merged(rows, 0, PART)
         r.o1[rows, :] = out
         r.m1[rows, :] = top
         r.l1[rows, :] = den
         return 0
 
-    lax.fori_loop(0, TILES, prior_first, 0)
+    lax.fori_loop(0, TILES // 2, prior_first, 0)
+    multiply_slab()
 
     for copy in keys_on(1):
         copy.wait()
     head_masks(r.vp, PART, PART)
 
-    def prior_second(i, _):
-        @pl.when(i == TILES - 1)
-        def _():
-            spread_fused()
-
-        rows = pl.ds(pl.multiple_of(i * ROWS, ROWS), ROWS)
-        out, top, den = merged(rows, PART)
+    def send_pooled(i, out, den):
         ctx = (out / den).astype(B16)
         pooled = dot(tile_pool, ctx).astype(B16)
         partial = dot(pooled, r.wo[...]).astype(B16)
@@ -417,22 +405,26 @@
             r.part[tt, prows, :] = partial[:, tt * FEAT : (tt + 1) * FEAT]
         for k in range(1, n_t):
             summed(i, k).start()
+
+    def prior_second(i, _):
+        rows = pl.ds(pl.multiple_of(i * ROWS, ROWS), ROWS)
+        out, _, den = merged(rows, PART, PART)
+        send_pooled(i, out, den)
         return 0
 
-    lax.fori_loop(0, TILES, prior_second, 0)
-
-    def summed_wait(i, _):
-        for k in range(1, n_t):
-            summed(i, k).wait()
+    def prior_whole(i, _):
+        @pl.when(i == TILES - 1)
+        def _():
+            spread_fused()
+
+        rows = pl.ds(pl.multiple_of(i * ROWS, ROWS), ROWS)
+        out, _, den = merged(rows, 0, PAD)
+        send_pooled(i, out, den)
         return 0
 
-    lax.fori_loop(0, TILES, summed_wait, 0)
-
-    total = r.part[t].astype(F32)
-    for k in range(1, n_t):
-        total = total + r.rs[t_other(k)].astype(F32)
-    pooled = (r.res[...] + total).astype(B16)
-    wide = jnp.concatenate([pooled, jnp.ones((POOLED, WIDE - FEAT), B16)], axis=1)
+    lax.fori_loop(0, TILES // 2, prior_second, 0)
+    lax.fori_loop(TILES // 2, TILES, prior_whole, 0)
+
     owners = jnp.broadcast_to(r.owners[...].astype(F32), (128, POOLED))
     same = jnp.transpose(owners)[:, 0:1] == owners[0:1, :]
     first = lax.broadcasted_iota(jnp.int32, (POOLED, POOLED), 0)
@@ -441,6 +433,19 @@
     target = owners[0:1, :] * SLOT + ordinal
     slot_row = lax.broadcasted_iota(jnp.int32, (n_tm * SLOT, POOLED), 0)
     place = jnp.where(slot_row.astype(F32) == target, 1.0, 0.0).astype(B16)
+
+    def summed_wait(i, _):
+        for k in range(1, n_t):
+            summed(i, k).wait()
+        return 0
+
+    lax.fori_loop(0, TILES, summed_wait, 0)
+
+    total = r.part[t].astype(F32)
+    for k in range(1, n_t):
+        total = total + r.rs[t_other(k)].astype(F32)
+    pooled = (r.res[...] + total).astype(B16)
+    wide = jnp.concatenate([pooled, jnp.ones((POOLED, WIDE - FEAT), B16)], axis=1)
     slots_ref, x_ref = r.slots, r.x
     slots_ref[...] = dot(place, wide).reshape(n_tm, SLOT, WIDE).astype(B16)
     x_ref[t, 0] = slots_ref[me]
@@ -458,6 +463,7 @@
         lax.fori_loop(max(1, g * members), (g + 1) * members, routed_start, 0)
 
     multiply_text()
+    ring_second(r.fall, "fz", "fm")
 
     def handed(g, k):
         rows = pl.ds(g * members, members)
@@ -487,48 +493,21 @@
         drain(x_ref.at[t, pl.ds(start, (g + 1) * members - start)], r.a2a_recv.at[g])
         for k in (1, -1):
             handed(g, k).start()
-        if g == 1:
-            ring_second(r.fall, "fz", "fm")
         if g > 0:
             relay(g - 1)
-    relay(GROUPS - 1)
-    drain(slots_ref.at[pl.ds(0, n_tm - 1)], r.a2a_send)
-    for k in range(1, NX):
-        text_sent(k).wait()
-    for g in range(GROUPS):
-        for k in (1, -1):
-            relayed(g, k).wait()
-
     used = SLOT - 1
     audio = n_tm * used
     fetched("rope").wait()
     srow = lax.broadcasted_iota(jnp.int32, (audio, n_tm * SLOT), 0)
     scol = lax.broadcasted_iota(jnp.int32, (audio, n_tm * SLOT), 1)
     source = (me - (scol >> 3)) & (n_tm - 1)
-    place = source * used + (scol & (SLOT - 1))
-    compact = jnp.where((place == srow) & ((scol & (SLOT - 1)) < used), 1.0, 0.0).astype(B16)
-    flags = None
-    for tt in range(n_t):
-        rows = x_ref[tt].astype(F32).reshape(n_tm * SLOT, WIDE).astype(B16)
-        rows = dot(compact, rows)
-        r.xc[:, tt * FEAT : (tt + 1) * FEAT] = rows[:, :FEAT].astype(B16)
-        if tt == 0:
-            flags = rows[:, FEAT : FEAT + 1]
-
-    adapted = dot(r.xc[...], r.adapter[...])
-    power = jnp.sum(adapted * adapted, axis=1, keepdims=True)
-    power = jnp.concatenate([power, jnp.zeros((SEQ - audio, 1), F32)], axis=0)
-    power = jnp.transpose(jnp.broadcast_to(power, (SEQ, 128)))
-    r.ss[t] = power[0:8, :]
-
-    def power_sent(k):
-        return remote(
-            r.ss.at[t], r.ss.at[t], r.ss_send.at[k - 1], r.ss_recv.at[k - 1], (me, t_other(k))
-        )
-
-    for k in range(1, n_t):
-        power_sent(k).start()
-
+    row_to = source * used + (scol & (SLOT - 1))
+    compact = jnp.where((row_to == srow) & ((scol & (SLOT - 1)) < used), 1.0, 0.0).astype(B16)
+
+    def flat(tt):
+        return x_ref[tt].astype(F32).reshape(n_tm * SLOT, WIDE).astype(B16)
+
+    flags = dot(compact, flat(t))[:, FEAT : FEAT + 1]
     present = jnp.concatenate([flags, jnp.ones((SEQ - audio, 1), F32)], axis=0)
     present = jnp.broadcast_to(present, (SEQ, 128))
     row = lax.broadcasted_iota(jnp.int32, (SEQ, SEQ), 0)
@@ -541,6 +520,32 @@
     cosine, sine = table[:, :LLM_HD], table[:, LLM_HD:]
     key_there = jnp.transpose(present)[0:1, :] > 0.5
     r.mask[...] = jnp.where(((col <= row) & key_there) | (col == row), 0.0, -1e30)
+
+    relay(GROUPS - 1)
+    drain(slots_ref.at[pl.ds(0, n_tm - 1)], r.a2a_send)
+    for k in range(1, NX):
+        text_sent(k).wait()
+    for g in range(GROUPS):
+        for k in (1, -1):
+            relayed(g, k).wait()
+
+    for tt in range(n_t):
+        rows = dot(compact, flat(tt))
+        r.xc[:, tt * FEAT : (tt + 1) * FEAT] = rows[:, :FEAT].astype(B16)
+
+    adapted = dot(r.xc[...], r.adapter[...])
+    power = jnp.sum(adapted * adapted, axis=1, keepdims=True)
+    power = jnp.concatenate([power, jnp.zeros((SEQ - audio, 1), F32)], axis=0)
+    power = jnp.transpose(jnp.broadcast_to(power, (SEQ, 128)))
+    r.ss[t] = power[0:8, :]
+
+    def power_sent(k):
+        return remote(
+            r.ss.at[t], r.ss.at[t], r.ss_send.at[k - 1], r.ss_recv.at[k - 1], (me, t_other(k))
+        )
+
+    for k in range(1, n_t):
+        power_sent(k).start()
 
     ring_last(r.fall, "fz", "fm")
     ring_done(r.fall, "fz", "fm")

time: 121 us -> 116 us (0.959)
  Pallas kernels: 117 us -> 112 us
    pallas_call x1, Pallas kernels: 117 us -> 112 us  [run_block(): pl.pallas_call(functools.partial(block_kernel, n_tm, n_t, names), out_sha...]
where the time goes in v2:
time: 116 us; the launch traced here: 115 us
  Pallas kernels  112 us (97%)
  local copies, waits for them, and re-layouts  3.73 us (3%)
    pallas_call x1, Pallas kernels, run_block(): pl.pallas_call(functools.partial(block_kernel, n_tm, n_t, names), out_sha...  112 us
    unnamed x3, local copies, waits for them, and re-layouts  3.07 us

profile of v2, /device:TPU:1, one launch (start us, length us, event | category | flops | bytes accessed | tf_op | source)
XLA Modules:
  0.0 115.5 jit_solution(7530311971981527234)
XLA Ops:
  0.0 0.0 copy-start
  0.0 0.9 copy-done
  0.9 0.1 dynamic-slice_reduce_fusion
  1.0 0.6 broadcast_in_dim.3.refs_9_
  1.6 111.7 %shard_map.172 = bf16[512,896]{1,0:T(8,128)(2,1)} custom-call(bf16[1500,1280]{1,0:T(8,128)(2,1)} %refs_0_.1, bf16[1280,256]{1,0:T(8,128)(2,1)} %refs_1_.1, bf16[1280,256]{1,0:T(8,128)(2,1)} %refs_2_.1, bf16[1280,256]{1,0:T(8,128)(2,1)} %refs_3_.1, bf16[1280,896]{1,0:T(8,128)(2,1)} %refs_4_.1, bf16[256,1280]{1,0:T(8,128)(2,1)} %refs_5_.1, ...), custom_call_target="tpu_custom_call" | custom-call | flops 20000000000 | bytes 20000000 | tf_op jit(solution)/shard_map/pallas_call | solution.py:676
  113.3 2.2 %copy.20 = bf16[512,896]{1,0:T(8,128)(2,1)} copy(bf16[512,896]{1,0:T(8,128)(2,1)} %shard_map.172) | data formatting | bytes 1835008
  (1 shorter events, 0.0 us)
Async XLA Ops:
  0.0 0.9 copy-start

commit v3 on v2

--- a/solution.py
+++ b/solution.py
@@ -289,6 +289,8 @@
                 r.tp[xv, :, to : to + PIECE] = text[:, lo : lo + PIECE]
     r.trow[xx] = r.tp[xx]
     ring_last(r.wz, "wz", "wm")
+    for k in range(1, NX):
+        text_rows(k).start()
     def fused_sent(k):
         return remote(
             r.fx.at[xx],
@@ -345,8 +347,6 @@
             total = total + r.fx[xv].astype(F32)
         r.fall[c, z] = total.astype(B16)
         ring_first(r.fall, "fz")
-        for k in range(1, NX):
-            text_rows(k).start()
 
     for copy in keys_on(0):
         copy.wait()
@@ -434,6 +434,8 @@
     slot_row = lax.broadcasted_iota(jnp.int32, (n_tm * SLOT, POOLED), 0)
     place = jnp.where(slot_row.astype(F32) == target, 1.0, 0.0).astype(B16)
 
+    multiply_text()
+
     def summed_wait(i, _):
         for k in range(1, n_t):
             summed(i, k).wait()
@@ -462,9 +464,6 @@
 
         lax.fori_loop(max(1, g * members), (g + 1) * members, routed_start, 0)
 
-    multiply_text()
-    ring_second(r.fall, "fz", "fm")
-
     def handed(g, k):
         rows = pl.ds(g * members, members)
         ref = x_ref.at[t, rows]
@@ -493,6 +492,8 @@
         drain(x_ref.at[t, pl.ds(start, (g + 1) * members - start)], r.a2a_recv.at[g])
         for k in (1, -1):
             handed(g, k).start()
+        if g == GROUPS - 1:
+            ring_second(r.fall, "fz", "fm")
         if g > 0:
             relay(g - 1)
     used = SLOT - 1

time: 116 us -> 118 us (1.017)
  Pallas kernels: 112 us -> 114 us
    pallas_call x1, Pallas kernels: 112 us -> 114 us  [run_block(): pl.pallas_call(functools.partial(block_kernel, n_tm, n_t, names), out_sha...]
where the time goes in v3:
time: 118 us
  Pallas kernels  114 us (97%)
  local copies, waits for them, and re-layouts  3.73 us (3%)
    pallas_call x1, Pallas kernels, run_block(): pl.pallas_call(functools.partial(block_kernel, n_tm, n_t, names), out_sha...  114 us
    unnamed x3, local copies, waits for them, and re-layouts  3.07 us

profile of v3, /device:TPU:1, one launch (start us, length us, event | category | flops | bytes accessed | tf_op | source)
XLA Modules:
  0.0 118.0 jit_solution(4001715561392724272)
XLA Ops:
  0.0 0.0 copy-start
  0.0 0.9 copy-done
  0.9 0.1 dynamic-slice_reduce_fusion
  1.0 0.6 broadcast_in_dim.3.refs_9_
  1.6 114.3 %shard_map.172 = bf16[512,896]{1,0:T(8,128)(2,1)} custom-call(bf16[1500,1280]{1,0:T(8,128)(2,1)} %refs_0_.1, bf16[1280,256]{1,0:T(8,128)(2,1)} %refs_1_.1, bf16[1280,256]{1,0:T(8,128)(2,1)} %refs_2_.1, bf16[1280,256]{1,0:T(8,128)(2,1)} %refs_3_.1, bf16[1280,896]{1,0:T(8,128)(2,1)} %refs_4_.1, bf16[256,1280]{1,0:T(8,128)(2,1)} %refs_5_.1, ...), custom_call_target="tpu_custom_call" | custom-call | flops 20000000000 | bytes 20000000 | tf_op jit(solution)/shard_map/pallas_call | solution.py:677
  115.8 2.2 %copy.20 = bf16[512,896]{1,0:T(8,128)(2,1)} copy(bf16[512,896]{1,0:T(8,128)(2,1)} %shard_map.172) | data formatting | bytes 1835008
  (1 shorter events, 0.0 us)
Async XLA Ops:
  0.0 0.9 copy-start
